TPU v7x, 256 devices: a whole 4x4x8 slice. The times are simulated.
256 devices in a mesh: patch: 64 (over x, z, core), feat: 4 (over y).
Axes of the slice: x: 4, y: 4, z: 8, core: 2. Of those that a mesh axis runs over, the one named last changes fastest.
Arguments:
- nodes: bfloat16 [40960, 512], P(('patch', 'feat')), may hold values from -6 to 6
- edges: bfloat16 [327680, 512], P(('patch', 'feat')), may hold values from -6 to 6
- receivers: int32 [327680], P(('patch', 'feat')), may hold values from 0 to 639
- sender_slot: int32 [327680], P(('patch', 'feat')), may hold values from 0 to 2175
- send_rows: int32 [64, 4, 64, 24], P('patch', 'feat'), may hold values from 0 to 159
- live_edges: int32 [256], P(('patch', 'feat')), may hold values from 1 to 1280, 245760 in all
- edge_w1: bfloat16 [1536, 512], replicated, may hold values from -0.15625 to 0.15625
- edge_b1: float32 [512], replicated, may hold values from -3 to 3
- edge_w2: bfloat16 [512, 512], replicated, may hold values from -0.25 to 0.25
- edge_gain: float32 [512], replicated, may hold values from 0.5 to 1.5
- node_w1: bfloat16 [1024, 512], replicated, may hold values from -0.1875 to 0.1875
- node_b1: float32 [512], replicated, may hold values from -3 to 3
- node_w2: bfloat16 [512, 512], replicated, may hold values from -0.25 to 0.25
- node_gain: float32 [512], replicated, may hold values from 0.5 to 1.5
Outputs:
- edges_out: bfloat16 [327680, 512], P(('patch', 'feat'))
- nodes_out: bfloat16 [40960, 512], P(('patch', 'feat'))
Inputs may be any that keep to these rules, and one draw needn't show every extreme that they name: `live_edges`: edge slots at or past a device's count are padding.
All inputs are finite; a program needn't handle non-finite values.
Results may differ from a plain program's by a relative error of at most 0.0052.
Values may be sent and summed in bfloat16 or wider, within the bound.
No kernel may reach another device: no remote copies, remote signals or barrier semaphores. Data moves between devices by JAX's collectives and lax.ppermute only.
A program may use at most 64 MiB of HBM per device.

v0:
```python
import jax
import jax.numpy as jnp
from jax import lax
from jax.sharding import PartitionSpec as P

epsilon = 1e-05


def cut_along(value, dim, size):
    lengths = value.shape
    tiles = value.reshape(*lengths[:dim], size, lengths[dim] // size, *lengths[dim + 1 :])
    return jnp.moveaxis(tiles, dim, 0)


def sum_at_owner(value, axis, dim):
    size = lax.axis_size(axis)
    tiles = lax.all_to_all(cut_along(value, dim, size), axis, 0, 0, tiled=True)
    return jnp.sum(tiles, axis=0)


def layer_norm(values, scales):
    average = jnp.mean(values, axis=-1, keepdims=True)
    centred = values - average
    variance = jnp.mean(centred * centred, axis=-1, keepdims=True)
    return centred * lax.rsqrt(variance + epsilon) * scales


def edge_change(edge_rows, sender_feat, receiver_feat, edge_w1, edge_b1, edge_w2, edge_gain):
    latent = edge_rows.shape[1]
    first = jnp.dot(edge_rows, edge_w1[:latent], preferred_element_type=jnp.float32)
    first = first + jnp.dot(
        sender_feat, edge_w1[latent : 2 * latent], preferred_element_type=jnp.float32
    )
    first = first + jnp.dot(
        receiver_feat, edge_w1[2 * latent :], preferred_element_type=jnp.float32
    )
    hidden = jax.nn.silu(first + edge_b1).astype(jnp.bfloat16)
    return layer_norm(jnp.dot(hidden, edge_w2, preferred_element_type=jnp.float32), edge_gain)


def node_change(node_rows, incoming, node_w1, node_b1, node_w2, node_gain):
    latent = node_rows.shape[1]
    first = jnp.dot(node_rows, node_w1[:latent], preferred_element_type=jnp.float32)
    first = first + jnp.dot(incoming, node_w1[latent:], preferred_element_type=jnp.float32)
    hidden = jax.nn.silu(first + node_b1).astype(jnp.bfloat16)
    return layer_norm(jnp.dot(hidden, node_w2, preferred_element_type=jnp.float32), node_gain)


def local(
    nodes,
    edges,
    receivers,
    sender_slot,
    send_rows,
    live_edges,
    edge_w1,
    edge_b1,
    edge_w2,
    edge_gain,
    node_w1,
    node_b1,
    node_w2,
    node_gain,
):
    latent = nodes.shape[1]
    edge_count = edges.shape[0]
    patch_rows = lax.all_gather(nodes, "feat", axis=0, tiled=True)
    patch_count = patch_rows.shape[0]
    outgoing = send_rows[0, 0]
    packed = jnp.take(nodes, outgoing.reshape(-1), axis=0).reshape(
        outgoing.shape[0], outgoing.shape[1], latent
    )
    remote = lax.all_to_all(packed, "patch", split_axis=0, concat_axis=0, tiled=True).reshape(
        -1, latent
    )
    lookup_rows = jnp.concatenate([patch_rows, remote], axis=0)
    sender_feat = jnp.take(lookup_rows, sender_slot, axis=0)
    receiver_feat = jnp.take(patch_rows, receivers, axis=0)
    alive_count = live_edges[0]
    alive = lax.broadcasted_iota(jnp.int32, (edge_count,), 0) < alive_count
    change = edge_change(edges, sender_feat, receiver_feat, edge_w1, edge_b1, edge_w2, edge_gain)
    edges_out = (edges.astype(jnp.float32) + jnp.where(alive[:, None], change, 0.0)).astype(
        jnp.bfloat16
    )
    owner_rows = lax.broadcasted_iota(jnp.int32, (patch_count, edge_count), 0)
    one_hot = ((receivers[None, :] == owner_rows) & alive[None, :]).astype(jnp.bfloat16)
    partial_sums = jnp.dot(one_hot, edges_out, preferred_element_type=jnp.float32)
    summed = sum_at_owner(partial_sums, "feat", 0)
    incoming = summed.astype(jnp.bfloat16)
    change = node_change(nodes, incoming, node_w1, node_b1, node_w2, node_gain)
    nodes_out = (nodes.astype(jnp.float32) + change).astype(jnp.bfloat16)
    return (edges_out, nodes_out)


def solution(mesh):
    placed = (
        P(("patch", "feat"), None),
        P(("patch", "feat"), None),
        P(("patch", "feat")),
        P(("patch", "feat")),
        P("patch", "feat", None, None),
        P(("patch", "feat")),
        P(),
        P(),
        P(),
        P(),
        P(),
        P(),
        P(),
        P(),
    )
    return jax.shard_map(
        local,
        mesh=mesh,
        in_specs=placed,
        out_specs=(P(("patch", "feat"), None), P(("patch", "feat"), None)),
        check_vma=False,
    )
```

profile of v0, /device:TPU:1, one launch (start us, length us, event | category | flops | bytes accessed | tf_op | source)
XLA Modules:
  0.0 107.9 jit_solution(567308543703744715)
XLA Ops:
  0.6 0.8 copy.21
  1.5 0.7 compare_and_fusion
  2.5 5.8 %gather_fusion = bf16[1536,512]{1,0:T(8,128)(2,1)S(1)} fusion(bf16[160,512]{1,0:T(8,128)(2,1)} %param.14, s32[2048]{0:T(1024)S(1)} %pad_clamp_fusion.2), kind=kCustom, calls=%fused_computation | custom fusion | bytes 3151872 | tf_op jit(solution)/shard_map/jit(_take)/gather | solution.py:70
  8.3 1.4 %broadcast_select_fusion = bf16[64,24,512]{2,1,0:T(8,128)(2,1)} fusion(bf16[64,24,512]{2,1,0:T(8,128)(2,1)S(1)} %bitcast.18, pred[64,24]{1,0:T(8,128)(4,1)S(1)} %copy.20), kind=kLoop, calls=%fused_computation.15 | loop fusion | flops 786432 | bytes 3147264 | tf_op jit(solution)/shard_map/jit(_take)/select_n | solution.py:70
  9.7 13.0 %all-to-all-start = ((bf16[64,24,512]{2,1,0:T(8,128)(2,1)}), bf16[64,24,512]{2,1,0:T(8,128)(2,1)S(1)}, u32[]{:S(2)}, u32[]{:S(2)}) async-start(bf16[64,24,512]{2,1,0:T(8,128)(2,1)} %broadcast_select_fusion), calls=%async_computation | async-start | bytes 3145728 | tf_op jit(solution)/shard_map/all_to_all | solution.py:73
  23.4 2.4 %copy.19 = bf16[1280,512]{0,1:T(8,128)(2,1)} copy(bf16[1280,512]{1,0:T(8,128)(2,1)} %param.15) | data formatting | bytes 2621440 | tf_op args[1]
  25.8 12.0 %all_gather.3 = bf16[640,512]{1,0:T(8,128)(2,1)S(1)} all-gather(bf16[160,512]{1,0:T(8,128)(2,1)S(1)} %copy-done.1), channel_id=1, replica_groups=mesh['patch'=64,'feat'=4] {'feat'}, dimensions={0}, use_global_device_ids=true | all-gather | bytes 819200 | tf_op jit(solution)/shard_map/all_gather | solution.py:67
  37.8 4.7 %gather_fusion.2 = bf16[1280,512]{1,0:T(8,128)(2,1)} fusion(bf16[640,512]{1,0:T(8,128)(2,1)S(1)} %all_gather.3, s32[2048]{0:T(1024)S(1)} %pad_clamp_fusion), kind=kCustom, calls=%fused_computation.2 | custom fusion | bytes 2626560 | tf_op jit(solution)/shard_map/jit(_take)/gather | solution.py:78
  42.6 3.8 %fusion.25 = f32[1280,512]{1,0:T(8,128)} fusion(bf16[1280,512]{1,0:T(8,128)(2,1)} %param.15, bf16[1536,512]{1,0:T(8,128)(2,1)} %param.20), kind=kOutput, calls=%fused_computation.32 | convolution fusion | flops 671088640 | bytes 4456448 | tf_op jit(solution)/shard_map/dot_general | solution.py:30
  46.4 16.0 %all-to-all-done = bf16[64,24,512]{2,1,0:T(8,128)(2,1)S(1)} async-done(((bf16[64,24,512]{2,1,0:T(8,128)(2,1)}), bf16[64,24,512]{2,1,0:T(8,128)(2,1)S(1)}, u32[]{:S(2)}, u32[]{:S(2)}) %all-to-all-start) | async-done | bytes 1572896 | tf_op jit(solution)/shard_map/all_to_all | solution.py:73
  62.5 1.5 %pad_maximum_fusion = bf16[2176,512]{1,0:T(8,128)(2,1)} fusion(bf16[1536,512]{1,0:T(8,128)(2,1)S(1)} %bitcast.17, bf16[640,512]{1,0:T(8,128)(2,1)S(1)} %all_gather.3), kind=kLoop, calls=%fused_computation.12 | loop fusion | flops 4456448 | bytes 4456448 | tf_op jit(solution)/shard_map/concatenate | solution.py:76
  64.0 6.9 %gather_fusion.1 = bf16[1280,512]{1,0:T(8,128)(2,1)} fusion(bf16[2176,512]{1,0:T(8,128)(2,1)} %pad_maximum_fusion, s32[2048]{0:T(1024)S(1)} %pad_clamp_fusion.1), kind=kCustom, calls=%fused_computation.1 | custom fusion | bytes 2626560 | tf_op jit(solution)/shard_map/jit(_take)/gather | solution.py:77
  70.9 3.9 %convolution_add_fusion.1 = f32[1280,512]{1,0:T(8,128)} fusion(f32[1280,512]{1,0:T(8,128)S(1)} %copy-done.2, bf16[1280,512]{1,0:T(8,128)(2,1)} %gather_fusion.1, pred[1280]{0:T(1024)(128)(4,1)S(1)} %compare_and_fusion.2, bf16[1536,512]{1,0:T(8,128)(2,1)} %param.20), kind=kOutput, calls=%fused_computation.5 | convolution fusion | flops 672399360 | bytes 7079168 | tf_op jit(solution)/shard_map/dot_general | solution.py:31
  74.7 4.1 %fusion.42 = (f32[1280]{0:T(1024)S(1)}, f32[1280,512]{0,1:T(8,128)S(1)}) fusion(bf16[512,512]{1,0:T(8,128)(2,1)S(1)} %copy-done, f32[1280,512]{1,0:T(8,128)} %convolution_add_fusion.1, f32[512]{0:T(512)S(1)} %copy-done.10, bf16[1280,512]{1,0:T(8,128)(2,1)} %gather_fusion.2, pred[1280]{0:T(1024)(128)(4,1)S(1)} %compare_and_fusion.1, bf16[1536,512]{1,0:T(8,128)(2,1)} %param.20), kind=kOutput, calls=%fused_computation.61 | convolution fusion | flops 1348074240 | bytes 7610624 | tf_op jit(solution)/shard_map/dot_general | solution.py:38
  78.9 0.3 multiply_reduce_fusion
  79.2 1.0 copy-done.3
  80.2 0.6 add_convert_fusion
  80.8 2.1 %fusion.2 = f32[640,512]{1,0:T(8,128)} fusion(bf16[1280,512]{0,1:T(8,128)(2,1)S(1)} %add_convert_fusion, s32[1280]{0:T(1024)S(1)} %copy-done.7, pred[1280]{0:T(1024)(128)(4,1)S(1)} %iota_compare_fusion.1), kind=kOutput, calls=%fused_computation.8 | convolution fusion | flops 840499200 | bytes 2627840 | tf_op jit(solution)/shard_map/dot_general | solution.py:87
  82.9 4.3 %all-to-all-start.1 = ((f32[4,160,512]{2,1,0:T(8,128)}), f32[4,160,512]{2,1,0:T(8,128)S(1)}, u32[]{:S(2)}, u32[]{:S(2)}) async-start(f32[4,160,512]{2,1,0:T(8,128)} %bitcast.19), calls=%async_computation.1 | async-start | bytes 2621440 | tf_op jit(solution)/shard_map/all_to_all | solution.py:17
  87.2 2.0 %fusion.20 = f32[160,512]{1,0:T(8,128)} fusion(bf16[160,512]{1,0:T(8,128)(2,1)S(1)} %copy-done.1, bf16[1024,512]{1,0:T(8,128)(2,1)} %param.24), kind=kOutput, calls=%fused_computation.28 | convolution fusion | flops 83886080 | bytes 1015808 | tf_op jit(solution)/shard_map/dot_general | solution.py:43
  89.3 1.5 %copy.22 = bf16[1280,512]{1,0:T(8,128)(2,1)} copy(bf16[1280,512]{0,1:T(8,128)(2,1)S(1)} %copy-done.5) | data formatting | bytes 2621440
  90.8 14.1 %all-to-all-done.1 = f32[4,160,512]{2,1,0:T(8,128)S(1)} async-done(((f32[4,160,512]{2,1,0:T(8,128)}), f32[4,160,512]{2,1,0:T(8,128)S(1)}, u32[]{:S(2)}, u32[]{:S(2)}) %all-to-all-start.1) | async-done | bytes 1310752 | tf_op jit(solution)/shard_map/all_to_all | solution.py:17
  105.0 1.9 %fusion.47 = (f32[160]{0:T(256)S(1)}, f32[160,512]{1,0:T(8,128)S(1)}) fusion(bf16[512,512]{1,0:T(8,128)(2,1)} %param.26, f32[160,512]{1,0:T(8,128)} %fusion.20, bf16[1024,512]{1,0:T(8,128)(2,1)} %param.24, f32[512]{0:T(512)S(1)} %copy-done.11, bf16[160,512]{1,0:T(8,128)(2,1)S(1)} %reduce_sum.47), kind=kOutput, calls=%fused_computation.62 | convolution fusion | flops 168427360 | bytes 1870464 | tf_op jit(solution)/shard_map/dot_general | solution.py:46
  107.1 0.8 add_convert_fusion.1
  (40 shorter events, 0.7 us)
Async XLA Ops:
  0.6 74.1 %copy-start = (bf16[512,512]{1,0:T(8,128)(2,1)S(1)}, bf16[512,512]{1,0:T(8,128)(2,1)}, u32[]{:S(2)}) copy-start(bf16[512,512]{1,0:T(8,128)(2,1)} %param.22) | copy-start | bytes 1572868
  9.7 52.8 %all-to-all-start = ((bf16[64,24,512]{2,1,0:T(8,128)(2,1)}), bf16[64,24,512]{2,1,0:T(8,128)(2,1)S(1)}, u32[]{:S(2)}, u32[]{:S(2)}) async-start(bf16[64,24,512]{2,1,0:T(8,128)(2,1)} %broadcast_select_fusion), calls=%async_computation | async-start | bytes 3145728 | tf_op jit(solution)/shard_map/all_to_all | solution.py:73
  22.7 3.1 %copy-start.7 = (s32[1280]{0:T(1024)S(1)}, s32[1280]{0:T(1024)}, u32[]{:S(2)}) copy-start(s32[1280]{0:T(1024)} %param.16) | copy-start | bytes 15364
  22.7 3.1 %copy-start.1 = (bf16[160,512]{1,0:T(8,128)(2,1)S(1)}, bf16[160,512]{1,0:T(8,128)(2,1)}, u32[]{:S(2)}) copy-start(bf16[160,512]{1,0:T(8,128)(2,1)} %param.14) | copy-start | bytes 491524
  37.8 4.7 %copy-start.6 = (s32[1280]{0:T(1024)S(1)}, s32[1280]{0:T(1024)}, u32[]{:S(2)}) copy-start(s32[1280]{0:T(1024)} %param.17) | copy-start | bytes 15364
  64.0 6.9 %copy-start.2 = (f32[1280,512]{1,0:T(8,128)S(1)}, f32[1280,512]{1,0:T(8,128)}, u32[]{:S(2)}) copy-start(f32[1280,512]{1,0:T(8,128)} %fusion.25) | copy-start | bytes 7864324
  70.9 3.9 %copy-start.10 = (f32[512]{0:T(512)S(1)}, f32[512]{0:T(512)}, u32[]{:S(2)}) copy-start(f32[512]{0:T(512)} %param.21) | copy-start | bytes 6148
  78.8 1.3 %copy-start.3 = (bf16[1280,512]{0,1:T(8,128)(2,1)S(1)}, bf16[1280,512]{0,1:T(8,128)(2,1)}, u32[]{:S(2)}) copy-start(bf16[1280,512]{0,1:T(8,128)(2,1)} %copy.19) | copy-start | bytes 3932164
  78.8 1.3 %copy-start.8 = (f32[512]{0:T(512)S(1)}, f32[512]{0:T(512)}, u32[]{:S(2)}) copy-start(f32[512]{0:T(512)} %param.23) | copy-start | bytes 6148
  80.8 2.1 %copy-start.4 = (bf16[1280,512]{0,1:T(8,128)(2,1)}, bf16[1280,512]{0,1:T(8,128)(2,1)S(1)}, u32[]{:S(2)}) copy-start(bf16[1280,512]{0,1:T(8,128)(2,1)S(1)} %add_convert_fusion) | copy-start | bytes 3932164
  82.9 6.3 %copy-start.5 = (bf16[1280,512]{0,1:T(8,128)(2,1)S(1)}, bf16[1280,512]{0,1:T(8,128)(2,1)}, u32[]{:S(2)}) copy-start(bf16[1280,512]{0,1:T(8,128)(2,1)} %copy-done.4) | copy-start | bytes 3932164
  82.9 21.9 %all-to-all-start.1 = ((f32[4,160,512]{2,1,0:T(8,128)}), f32[4,160,512]{2,1,0:T(8,128)S(1)}, u32[]{:S(2)}, u32[]{:S(2)}) async-start(f32[4,160,512]{2,1,0:T(8,128)} %bitcast.19), calls=%async_computation.1 | async-start | bytes 2621440 | tf_op jit(solution)/shard_map/all_to_all | solution.py:17
  89.3 15.7 %copy-start.11 = (f32[512]{0:T(512)S(1)}, f32[512]{0:T(512)}, u32[]{:S(2)}) copy-start(f32[512]{0:T(512)} %param.25) | copy-start | bytes 6148
  105.0 2.1 %copy-start.9 = (f32[512]{0:T(512)S(1)}, f32[512]{0:T(512)}, u32[]{:S(2)}) copy-start(f32[512]{0:T(512)} %param.27) | copy-start | bytes 6148
where the time goes:
time: 108 us
  waiting for transfers between devices  30.1 us (28%)
  local copies, waits for them, and re-layouts  23.4 us (22%)
  matrix products  17.8 us (16%)
  starting transfers between devices  17.3 us (16%)
  blocking collectives  12 us (11%)
  other arithmetic  5.84 us (5%)
  between operations  1.51 us (1%)
    all_to_all x1, waiting for transfers between devices, local(): lax.all_to_all(packed, 'patch', split_axis=0, concat_axis=0, tiled=True)  16 us
    all_to_all x1, waiting for transfers between devices, sum_at_owner(): tiles = lax.all_to_all(cut_along(value, dim, size), axis, 0, 0, tiled=True)  14.1 us
    all_to_all x1, starting transfers between devices, local(): lax.all_to_all(packed, 'patch', split_axis=0, concat_axis=0, tiled=True)  13 us
    all_gather x1, blocking collectives, local(): patch_rows = lax.all_gather(nodes, 'feat', axis=0, tiled=True)  12 us
    gather x1, local copies, waits for them, and re-layouts, local(): sender_feat = jnp.take(lookup_rows, sender_slot, axis=0)  6.87 us
    gather x1, local copies, waits for them, and re-layouts, local(): jnp.take(nodes, outgoing.reshape(-1), axis=0)  5.8 us
    unnamed x27, local copies, waits for them, and re-layouts  5.78 us
    gather x1, local copies, waits for them, and re-layouts, local(): receiver_feat = jnp.take(patch_rows, receivers, axis=0)  4.72 us
  transfers between devices with their start and end apart: 2, of which 2 were waited for; matrix products, arithmetic and copies ran while one was open for 13% of the time, Pallas kernels for 0%

commit v1 on v0

--- a/solution.py
+++ b/solution.py
@@ -64,7 +64,9 @@
 ):
     latent = nodes.shape[1]
     edge_count = edges.shape[0]
-    patch_rows = lax.all_gather(nodes, "feat", axis=0, tiled=True)
+    patch_rows = jnp.concatenate(
+        lax.all_to_all(jnp.stack([nodes] * lax.axis_size("feat")), "feat", 0, 0), axis=0
+    )
     patch_count = patch_rows.shape[0]
     outgoing = send_rows[0, 0]
     packed = jnp.take(nodes, outgoing.reshape(-1), axis=0).reshape(

time: 108 us -> 116 us (1.074)
  waiting for transfers between devices: 30.1 us -> 44.8 us
  blocking collectives: 12 us -> 0 us
  starting transfers between devices: 17.3 us -> 23.1 us
    all_to_all x1, waiting for transfers between devices: 16 us -> 28.1 us  [local(): lax.all_to_all(packed, 'patch', split_axis=0, concat_axis=0, tiled=True)]
    all_gather x1 -> x0, blocking collectives: 12 us -> none  [local(): patch_rows = lax.all_gather(nodes, 'feat', axis=0, tiled=True)]
    all_to_all x0 -> x1, starting transfers between devices: none -> 5.01 us  [local(): lax.all_to_all(jnp.stack([nodes] * lax.axis_size('feat')), 'feat', 0, 0)]
    all_to_all x0 -> x1, waiting for transfers between devices: none -> 2.34 us  [local(): lax.all_to_all(jnp.stack([nodes] * lax.axis_size('feat')), 'feat', 0, 0)]
    another operation x0 -> x1, local copies, waits for them, and re-layouts: none -> 1.88 us  [local(): jnp.stack([nodes] * lax.axis_size('feat'))]
    all_to_all x1, starting transfers between devices: 13 us -> 14.4 us  [local(): lax.all_to_all(packed, 'patch', split_axis=0, concat_axis=0, tiled=True)]
    unnamed x27 -> x29, local copies, waits for them, and re-layouts: 5.78 us -> 5.02 us
  transfers between devices with their start and end apart: 2 -> 3, of which waited for: 2 -> 3; matrix products, arithmetic and copies ran while one was open for 13% -> 18% of each run, Pallas kernels for 0% -> 0%
where the time goes in v1:
time: 116 us
  waiting for transfers between devices  44.8 us (39%)
  local copies, waits for them, and re-layouts  23.5 us (20%)
  starting transfers between devices  23.1 us (20%)
  matrix products  17.8 us (15%)
  other arithmetic  5.12 us (4%)
  between operations  1.54 us (1%)
    all_to_all x1, waiting for transfers between devices, local(): lax.all_to_all(packed, 'patch', split_axis=0, concat_axis=0, tiled=True)  28.1 us
    all_to_all x1, starting transfers between devices, local(): lax.all_to_all(packed, 'patch', split_axis=0, concat_axis=0, tiled=True)  14.4 us
    all_to_all x1, waiting for transfers between devices, sum_at_owner(): tiles = lax.all_to_all(cut_along(value, dim, size), axis, 0, 0, tiled=True)  14.4 us
    gather x1, local copies, waits for them, and re-layouts, local(): sender_feat = jnp.take(lookup_rows, sender_slot, axis=0)  6.85 us
    unnamed x29, local copies, waits for them, and re-layouts  5.02 us
    all_to_all x1, starting transfers between devices, local(): lax.all_to_all(jnp.stack([nodes] * lax.axis_size('feat')), 'feat', 0, 0)  5.01 us
    gather x1, local copies, waits for them, and re-layouts, local(): jnp.take(nodes, outgoing.reshape(-1), axis=0)  4.81 us
    gather x1, local copies, waits for them, and re-layouts, local(): receiver_feat = jnp.take(patch_rows, receivers, axis=0)  4.71 us
  transfers between devices with their start and end apart: 3, of which 3 were waited for; matrix products, arithmetic and copies ran while one was open for 18% of the time, Pallas kernels for 0%

profile of v1, /device:TPU:1, one launch (start us, length us, event | category | flops | bytes accessed | tf_op | source)
XLA Modules:
  0.0 115.7 jit_solution(7735684478757411605)
XLA Ops:
  0.7 1.9 %stack.2 = bf16[4,160,512]{2,1,0:T(8,128)(2,1)} broadcast(bf16[160,512]{1,0:T(8,128)(2,1)} %param.14), dimensions={1,2} | broadcast | bytes 819200 | tf_op jit(solution)/shard_map/stack | solution.py:68
  2.5 5.0 %all-to-all-start = ((bf16[4,160,512]{2,1,0:T(8,128)(2,1)}), bf16[4,160,512]{2,1,0:T(8,128)(2,1)S(1)}, u32[]{:S(2)}, u32[]{:S(2)}) async-start(bf16[4,160,512]{2,1,0:T(8,128)(2,1)} %stack.2), calls=%async_computation | async-start | bytes 1310720 | tf_op jit(solution)/shard_map/all_to_all | solution.py:68
  7.8 4.8 %gather_fusion = bf16[1536,512]{1,0:T(8,128)(2,1)S(1)} fusion(bf16[160,512]{1,0:T(8,128)(2,1)S(1)} %copy-done.1, s32[2048]{0:T(1024)S(1)} %pad_clamp_fusion.2), kind=kCustom, calls=%fused_computation | custom fusion | bytes 3151872 | tf_op jit(solution)/shard_map/jit(_take)/gather | solution.py:72
  12.7 1.4 %broadcast_select_fusion = bf16[64,24,512]{2,1,0:T(8,128)(2,1)} fusion(bf16[64,24,512]{2,1,0:T(8,128)(2,1)S(1)} %bitcast.21, pred[64,24]{1,0:T(8,128)(4,1)S(1)} %copy.20), kind=kLoop, calls=%fused_computation.15 | loop fusion | flops 786432 | bytes 3147264 | tf_op jit(solution)/shard_map/jit(_take)/select_n | solution.py:72
  14.2 2.3 %all-to-all-done = bf16[4,160,512]{2,1,0:T(8,128)(2,1)S(1)} async-done(((bf16[4,160,512]{2,1,0:T(8,128)(2,1)}), bf16[4,160,512]{2,1,0:T(8,128)(2,1)S(1)}, u32[]{:S(2)}, u32[]{:S(2)}) %all-to-all-start) | async-done | bytes 655392 | tf_op jit(solution)/shard_map/all_to_all | solution.py:68
  16.5 14.4 %all-to-all-start.1 = ((bf16[64,24,512]{2,1,0:T(8,128)(2,1)}), bf16[64,24,512]{2,1,0:T(8,128)(2,1)S(1)}, u32[]{:S(2)}, u32[]{:S(2)}) async-start(bf16[64,24,512]{2,1,0:T(8,128)(2,1)} %broadcast_select_fusion), calls=%async_computation.1 | async-start | bytes 3145728 | tf_op jit(solution)/shard_map/all_to_all | solution.py:75
  31.6 2.4 %copy.19 = bf16[1280,512]{0,1:T(8,128)(2,1)} copy(bf16[1280,512]{1,0:T(8,128)(2,1)} %param.15) | data formatting | bytes 2621440 | tf_op args[1]
  34.1 3.8 %fusion.25 = f32[1280,512]{1,0:T(8,128)} fusion(bf16[1280,512]{1,0:T(8,128)(2,1)} %param.15, bf16[1536,512]{1,0:T(8,128)(2,1)} %param.20), kind=kOutput, calls=%fused_computation.32 | convolution fusion | flops 671088640 | bytes 4456448 | tf_op jit(solution)/shard_map/dot_general | solution.py:30
  37.9 4.7 %gather_fusion.2 = bf16[1280,512]{1,0:T(8,128)(2,1)} fusion(bf16[640,512]{1,0:T(8,128)(2,1)S(1)} %bitcast.18, s32[2048]{0:T(1024)S(1)} %pad_clamp_fusion), kind=kCustom, calls=%fused_computation.2 | custom fusion | bytes 2626560 | tf_op jit(solution)/shard_map/jit(_take)/gather | solution.py:80
  42.6 28.1 %all-to-all-done.1 = bf16[64,24,512]{2,1,0:T(8,128)(2,1)S(1)} async-done(((bf16[64,24,512]{2,1,0:T(8,128)(2,1)}), bf16[64,24,512]{2,1,0:T(8,128)(2,1)S(1)}, u32[]{:S(2)}, u32[]{:S(2)}) %all-to-all-start.1) | async-done | bytes 1572896 | tf_op jit(solution)/shard_map/all_to_all | solution.py:75
  70.7 1.5 %pad_maximum_fusion = bf16[2176,512]{1,0:T(8,128)(2,1)} fusion(bf16[1536,512]{1,0:T(8,128)(2,1)S(1)} %bitcast.20, bf16[640,512]{1,0:T(8,128)(2,1)S(1)} %bitcast.19), kind=kLoop, calls=%fused_computation.12 | loop fusion | flops 4456448 | bytes 4456448 | tf_op jit(solution)/shard_map/concatenate | solution.py:78
  72.2 6.9 %gather_fusion.1 = bf16[1280,512]{1,0:T(8,128)(2,1)} fusion(bf16[2176,512]{1,0:T(8,128)(2,1)} %pad_maximum_fusion, s32[2048]{0:T(1024)S(1)} %pad_clamp_fusion.1), kind=kCustom, calls=%fused_computation.1 | custom fusion | bytes 2626560 | tf_op jit(solution)/shard_map/jit(_take)/gather | solution.py:79
  79.0 3.9 %convolution_add_fusion.1 = f32[1280,512]{1,0:T(8,128)} fusion(f32[1280,512]{1,0:T(8,128)S(1)} %copy-done.2, bf16[1280,512]{1,0:T(8,128)(2,1)} %gather_fusion.1, pred[1280]{0:T(1024)(128)(4,1)S(1)} %compare_and_fusion.2, bf16[1536,512]{1,0:T(8,128)(2,1)} %param.20), kind=kOutput, calls=%fused_computation.5 | convolution fusion | flops 672399360 | bytes 7079168 | tf_op jit(solution)/shard_map/dot_general | solution.py:31
  82.9 4.1 %fusion.42 = (f32[1280]{0:T(1024)S(1)}, f32[1280,512]{0,1:T(8,128)S(1)}) fusion(bf16[512,512]{1,0:T(8,128)(2,1)S(1)} %copy-done, f32[1280,512]{1,0:T(8,128)} %convolution_add_fusion.1, f32[512]{0:T(512)S(1)} %copy-done.11, bf16[1280,512]{1,0:T(8,128)(2,1)} %gather_fusion.2, pred[1280]{0:T(1024)(128)(4,1)S(1)} %compare_and_fusion.1, bf16[1536,512]{1,0:T(8,128)(2,1)} %param.20), kind=kOutput, calls=%fused_computation.61 | convolution fusion | flops 1348074240 | bytes 7610624 | tf_op jit(solution)/shard_map/dot_general | solution.py:38
  87.0 0.3 multiply_reduce_fusion
  87.4 1.0 copy-done.3
  88.3 0.6 add_convert_fusion
  89.0 2.1 %fusion.2 = f32[640,512]{1,0:T(8,128)} fusion(bf16[1280,512]{0,1:T(8,128)(2,1)S(1)} %add_convert_fusion, s32[1280]{0:T(1024)S(1)} %copy-done.8, pred[1280]{0:T(1024)(128)(4,1)S(1)} %iota_compare_fusion.1), kind=kOutput, calls=%fused_computation.8 | convolution fusion | flops 840499200 | bytes 2627840 | tf_op jit(solution)/shard_map/dot_general | solution.py:89
  91.1 3.7 %all-to-all-start.2 = ((f32[4,160,512]{2,1,0:T(8,128)}), f32[4,160,512]{2,1,0:T(8,128)S(1)}, u32[]{:S(2)}, u32[]{:S(2)}) async-start(f32[4,160,512]{2,1,0:T(8,128)} %bitcast.22), calls=%async_computation.2 | async-start | bytes 2621440 | tf_op jit(solution)/shard_map/all_to_all | solution.py:17
  94.8 2.0 %fusion.20 = f32[160,512]{1,0:T(8,128)} fusion(bf16[160,512]{1,0:T(8,128)(2,1)S(1)} %copy-done.1, bf16[1024,512]{1,0:T(8,128)(2,1)} %param.24), kind=kOutput, calls=%fused_computation.28 | convolution fusion | flops 83886080 | bytes 1015808 | tf_op jit(solution)/shard_map/dot_general | solution.py:43
  96.8 1.5 %copy.22 = bf16[1280,512]{1,0:T(8,128)(2,1)} copy(bf16[1280,512]{0,1:T(8,128)(2,1)S(1)} %copy-done.5) | data formatting | bytes 2621440
  98.3 14.4 %all-to-all-done.2 = f32[4,160,512]{2,1,0:T(8,128)S(1)} async-done(((f32[4,160,512]{2,1,0:T(8,128)}), f32[4,160,512]{2,1,0:T(8,128)S(1)}, u32[]{:S(2)}, u32[]{:S(2)}) %all-to-all-start.2) | async-done | bytes 1310752 | tf_op jit(solution)/shard_map/all_to_all | solution.py:17
  112.8 1.9 %fusion.47 = (f32[160]{0:T(256)S(1)}, f32[160,512]{1,0:T(8,128)S(1)}) fusion(bf16[512,512]{1,0:T(8,128)(2,1)} %param.26, f32[160,512]{1,0:T(8,128)} %fusion.20, bf16[1024,512]{1,0:T(8,128)(2,1)} %param.24, f32[512]{0:T(512)S(1)} %copy-done.12, bf16[160,512]{1,0:T(8,128)(2,1)S(1)} %reduce_sum.47), kind=kOutput, calls=%fused_computation.62 | convolution fusion | flops 168427360 | bytes 1870464 | tf_op jit(solution)/shard_map/dot_general | solution.py:46
  114.9 0.8 add_convert_fusion.1
  (44 shorter events, 0.8 us)
Async XLA Ops:
  0.6 82.3 %copy-start = (bf16[512,512]{1,0:T(8,128)(2,1)S(1)}, bf16[512,512]{1,0:T(8,128)(2,1)}, u32[]{:S(2)}) copy-start(bf16[512,512]{1,0:T(8,128)(2,1)} %param.22) | copy-start | bytes 1572868
  0.6 7.1 %copy-start.1 = (bf16[160,512]{1,0:T(8,128)(2,1)S(1)}, bf16[160,512]{1,0:T(8,128)(2,1)}, u32[]{:S(2)}) copy-start(bf16[160,512]{1,0:T(8,128)(2,1)} %param.14) | copy-start | bytes 491524
  0.7 6.9 %copy-start.6 = (s32[1,1,64,24]{2,3,1,0:T(8,128)S(1)}, s32[1,1,64,24]{2,3,1,0:T(8,128)}, u32[]{:S(2)}) copy-start(s32[1,1,64,24]{2,3,1,0:T(8,128)} %param.18) | copy-start | bytes 18436
  2.5 13.9 %all-to-all-start = ((bf16[4,160,512]{2,1,0:T(8,128)(2,1)}), bf16[4,160,512]{2,1,0:T(8,128)(2,1)S(1)}, u32[]{:S(2)}, u32[]{:S(2)}) async-start(bf16[4,160,512]{2,1,0:T(8,128)(2,1)} %stack.2), calls=%async_computation | async-start | bytes 1310720 | tf_op jit(solution)/shard_map/all_to_all | solution.py:68
  16.5 54.2 %all-to-all-start.1 = ((bf16[64,24,512]{2,1,0:T(8,128)(2,1)}), bf16[64,24,512]{2,1,0:T(8,128)(2,1)S(1)}, u32[]{:S(2)}, u32[]{:S(2)}) async-start(bf16[64,24,512]{2,1,0:T(8,128)(2,1)} %broadcast_select_fusion), calls=%async_computation.1 | async-start | bytes 3145728 | tf_op jit(solution)/shard_map/all_to_all | solution.py:75
  30.9 3.1 %copy-start.7 = (s32[1280]{0:T(1024)S(1)}, s32[1280]{0:T(1024)}, u32[]{:S(2)}) copy-start(s32[1280]{0:T(1024)} %param.17) | copy-start | bytes 15364
  30.9 3.1 %copy-start.8 = (s32[1280]{0:T(1024)S(1)}, s32[1280]{0:T(1024)}, u32[]{:S(2)}) copy-start(s32[1280]{0:T(1024)} %param.16) | copy-start | bytes 15364
  72.2 6.9 %copy-start.2 = (f32[1280,512]{1,0:T(8,128)S(1)}, f32[1280,512]{1,0:T(8,128)}, u32[]{:S(2)}) copy-start(f32[1280,512]{1,0:T(8,128)} %fusion.25) | copy-start | bytes 7864324
  79.0 3.9 %copy-start.11 = (f32[512]{0:T(512)S(1)}, f32[512]{0:T(512)}, u32[]{:S(2)}) copy-start(f32[512]{0:T(512)} %param.21) | copy-start | bytes 6148
  87.0 1.3 %copy-start.3 = (bf16[1280,512]{0,1:T(8,128)(2,1)S(1)}, bf16[1280,512]{0,1:T(8,128)(2,1)}, u32[]{:S(2)}) copy-start(bf16[1280,512]{0,1:T(8,128)(2,1)} %copy.19) | copy-start | bytes 3932164
  87.0 1.3 %copy-start.9 = (f32[512]{0:T(512)S(1)}, f32[512]{0:T(512)}, u32[]{:S(2)}) copy-start(f32[512]{0:T(512)} %param.23) | copy-start | bytes 6148
  89.0 2.1 %copy-start.4 = (bf16[1280,512]{0,1:T(8,128)(2,1)}, bf16[1280,512]{0,1:T(8,128)(2,1)S(1)}, u32[]{:S(2)}) copy-start(bf16[1280,512]{0,1:T(8,128)(2,1)S(1)} %add_convert_fusion) | copy-start | bytes 3932164
  91.1 5.7 %copy-start.5 = (bf16[1280,512]{0,1:T(8,128)(2,1)S(1)}, bf16[1280,512]{0,1:T(8,128)(2,1)}, u32[]{:S(2)}) copy-start(bf16[1280,512]{0,1:T(8,128)(2,1)} %copy-done.4) | copy-start | bytes 3932164
  91.1 21.5 %all-to-all-start.2 = ((f32[4,160,512]{2,1,0:T(8,128)}), f32[4,160,512]{2,1,0:T(8,128)S(1)}, u32[]{:S(2)}, u32[]{:S(2)}) async-start(f32[4,160,512]{2,1,0:T(8,128)} %bitcast.22), calls=%async_computation.2 | async-start | bytes 2621440 | tf_op jit(solution)/shard_map/all_to_all | solution.py:17
  96.8 16.0 %copy-start.12 = (f32[512]{0:T(512)S(1)}, f32[512]{0:T(512)}, u32[]{:S(2)}) copy-start(f32[512]{0:T(512)} %param.25) | copy-start | bytes 6148
  112.8 2.1 %copy-start.10 = (f32[512]{0:T(512)S(1)}, f32[512]{0:T(512)}, u32[]{:S(2)}) copy-start(f32[512]{0:T(512)} %param.27) | copy-start | bytes 6148
